TPU v7x, 128 devices: a whole 4x4x4 slice. The times are simulated.
128 devices in a mesh: pipe: 2 (over y_hi), seq: 16 (over x, z), dp: 4 (over y_lo, core).
Axes of the slice: x: 4, y: 4 (y_hi: 2, y_lo: 2; y = y_hi * 2 + y_lo), z: 4, core: 2. Of those that a mesh axis runs over, the one named last changes fastest.
Arguments:
- queries: bfloat16 [2, 4, 16, 384, 1536], P('pipe', 'dp', 'seq'), may hold values from -18 to 18
- keys: bfloat16 [2, 4, 16, 384, 1536], P('pipe', 'dp', 'seq'), may hold values from -18 to 18
- values: bfloat16 [2, 4, 16, 384, 1536], P('pipe', 'dp', 'seq'), may hold values from -6 to 6
- grad_out: bfloat16 [2, 4, 16, 384, 1536], P('pipe', 'dp', 'seq'), may hold values from -20 to 20
- norm_gains: float32 [2, 2, 128], P('pipe'), may hold values from 0.5 to 1.5
- kv_tiles: int32 [2, 4, 16, 3], P('pipe', 'dp', 'seq'), may hold values from -1 to 15, as said below
Outputs:
- qkv_grad: bfloat16 [2, 3, 4, 16, 384, 1536], P('pipe', None, 'dp', 'seq')
- gain_grads: float32 [2, 2, 128], P('pipe')
Inputs may be any that keep to these rules, and one draw needn't show every extreme that they name: `kv_tiles`: tile t covers frame tile t // 1 and spatial tile t % 1. The row of tile t names tile t itself and some of the other tiles of frame tiles t - 1, t // 1 and t + 1 inside the sample, each at most once, in some order; its other entries are -1.
All inputs are finite; a program needn't handle non-finite values.
Results may differ from a plain program's by a relative error of at most 0.007.
Values may be sent and summed in bfloat16 or wider, within the bound.
A program may use at most 256 MiB of HBM per device.

v0:
```python
import math
import jax
import jax.numpy as jnp
from jax import lax
from jax.sharding import PartitionSpec as P

HEADS = 12
HEAD_DIM = 128
epsilon = 1e-06


def padded(shard, sides, width):
    for axis, dim in sides:
        size, length = (lax.axis_size(axis), shard.shape[dim])
        up = [(i, (i + 1) % size) for i in range(size - 1)]
        down = [(j, i) for i, j in up]
        last = lax.slice_in_dim(shard, length - width, length, axis=dim)
        initial = lax.slice_in_dim(shard, 0, width, axis=dim)
        before = lax.ppermute(last, axis, up)
        after = lax.ppermute(initial, axis, down)
        shard = jnp.concatenate([before, shard, after], axis=dim)
    return shard


def passed_along(value, axis, steps):
    count = lax.axis_size(axis)
    initial, last = (max(0, -steps), min(count, count - steps))
    return lax.ppermute(value, axis, [(source, source + steps) for source in range(initial, last)])


def passed_along_2(value, axis, steps):
    count = lax.axis_size(axis)
    pairs = [(source, (source + steps) % count) for source in range(count)]
    return lax.ppermute(value, axis, pairs)


def normalize(source, gain_row):
    floats = source.astype(jnp.float32).reshape(source.shape[:-1] + (HEADS, HEAD_DIM))
    scaled = lax.rsqrt(jnp.mean(floats * floats, axis=-1, keepdims=True) + epsilon)
    normed = (floats * scaled * gain_row).astype(jnp.bfloat16).reshape(source.shape)
    return (normed, floats, scaled)


def norm_back(grad_hat, floats, scaled, gain_row):
    projected = jnp.sum(gain_row * grad_hat * floats, axis=-1, keepdims=True)
    gradient = scaled * gain_row * grad_hat - scaled**3 * floats * projected / HEAD_DIM
    gain_part = jnp.sum((grad_hat * floats * scaled).reshape(-1, HEAD_DIM), axis=0)
    return (gradient.reshape(gradient.shape[:-2] + (HEADS * HEAD_DIM,)), gain_part)


def score_block(query_head, grad_head, key_head, value_head, key_mask):
    root_scale = HEAD_DIM ** (-0.5)
    scores = (
        jnp.einsum("nqhd,nkhd->nhqk", query_head, key_head, preferred_element_type=jnp.float32)
        * root_scale
    )
    exp_scores = jnp.exp(scores) * key_mask[:, None, None, :]
    grad_attn = jnp.einsum(
        "nqhd,nkhd->nhqk", grad_head, value_head, preferred_element_type=jnp.float32
    )
    totals = jnp.sum(exp_scores, axis=-1, keepdims=True)
    attention = exp_scores / totals
    deltas = jnp.sum(attention * grad_attn, axis=-1, keepdims=True)
    dscore = (attention * (grad_attn - deltas)).astype(jnp.bfloat16)
    return (dscore, attention.astype(jnp.bfloat16), totals, deltas)


def spread(slot_grad, targets, list_slots, target_span):
    row_count, key_rows, head_count, head_width = slot_grad.shape
    shaped = slot_grad.reshape(
        row_count * list_slots, key_rows // list_slots, head_count * head_width
    )
    flat_targets = targets.reshape(-1)
    placed = jnp.where(flat_targets >= 0, flat_targets, target_span)
    totals = jnp.zeros(
        (target_span + 1, key_rows // list_slots, head_count * head_width), jnp.float32
    )
    return totals.at[placed].add(shaped)[:target_span]


def tile_pass(
    query_hat, grad_in, key_gathered, value_gathered, key_mask, targets, list_slots, target_span
):
    row_count, tile_rows, lane_total = query_hat.shape
    key_rows = key_gathered.shape[1]
    root_scale = HEAD_DIM ** (-0.5)
    query_parts, key_parts, value_parts, total_parts, delta_parts = ([], [], [], [], [])
    for first_head in range(0, HEADS, 2):
        lane_span = slice(first_head * HEAD_DIM, (first_head + 2) * HEAD_DIM)
        query_head = query_hat[:, :, lane_span].reshape(row_count, tile_rows, 2, HEAD_DIM)
        grad_head = grad_in[:, :, lane_span].reshape(row_count, tile_rows, 2, HEAD_DIM)
        key_head = key_gathered[:, :, lane_span].reshape(row_count, key_rows, 2, HEAD_DIM)
        value_head = value_gathered[:, :, lane_span].reshape(row_count, key_rows, 2, HEAD_DIM)
        dscore, attn_low, totals, deltas = score_block(
            query_head, grad_head, key_head, value_head, key_mask
        )
        query_parts.append(
            jnp.einsum("nhqk,nkhd->nqhd", dscore, key_head, preferred_element_type=jnp.float32)
            * root_scale
        )
        key_slot = (
            jnp.einsum("nhqk,nqhd->nkhd", dscore, query_head, preferred_element_type=jnp.float32)
            * root_scale
        )
        value_slot = jnp.einsum(
            "nhqk,nqhd->nkhd", attn_low, grad_head, preferred_element_type=jnp.float32
        )
        key_parts.append(spread(key_slot, targets, list_slots, target_span))
        value_parts.append(spread(value_slot, targets, list_slots, target_span))
        total_parts.append(totals[..., 0])
        delta_parts.append(deltas[..., 0])
    query_grads = jnp.concatenate(query_parts, axis=2)
    return (
        query_grads,
        jnp.concatenate(key_parts, axis=-1),
        jnp.concatenate(value_parts, axis=-1),
        jnp.concatenate(total_parts, axis=1),
        jnp.concatenate(delta_parts, axis=1),
    )


def local(queries, keys, values, grad_out, norm_gains, kv_tiles):
    query_in = queries[0, 0]
    key_in = keys[0, 0]
    value_in = values[0, 0]
    grad_in = grad_out[0, 0]
    gain_rows = norm_gains[0]
    tile_lists = kv_tiles[0, 0]
    tiles_here, tile_rows, lane_total = query_in.shape
    list_slots = tile_lists.shape[1]
    position = lax.axis_index("seq")
    seq_count = lax.axis_size("seq")
    query_hat, query_floats, query_scale = normalize(query_in, gain_rows[0])
    key_hat, key_floats, key_scale = normalize(key_in, gain_rows[1])
    rim_pairs = padded(jnp.stack([key_hat, value_in]), (("seq", 1),), tiles_here)
    live_slots = tile_lists >= 0
    key_mask = jnp.repeat(live_slots.astype(jnp.float32), tile_rows, axis=1)
    local_ids = tile_lists - (position - 1) * tiles_here
    fetch_ids = jnp.clip(local_ids, 0, 3 * tiles_here - 1)
    key_gathered = rim_pairs[0][fetch_ids].reshape(tiles_here, list_slots * tile_rows, lane_total)
    value_gathered = rim_pairs[1][fetch_ids].reshape(tiles_here, list_slots * tile_rows, lane_total)
    targets = jnp.where(live_slots, local_ids, -1)
    target_span = 3 * tiles_here
    query_hat_grad, key_acc, value_acc, totals, deltas = tile_pass(
        query_hat, grad_in, key_gathered, value_gathered, key_mask, targets, list_slots, target_span
    )
    query_grad, query_gain = norm_back(query_hat_grad, query_floats, query_scale, gain_rows[0])
    query_low = query_grad.astype(jnp.bfloat16)
    from_right = passed_along(jnp.stack([key_acc[:tiles_here], value_acc[:tiles_here]]), "seq", -1)
    from_left = passed_along(
        jnp.stack([key_acc[2 * tiles_here :], value_acc[2 * tiles_here :]]), "seq", 1
    )
    key_hat_grad = key_acc[tiles_here : 2 * tiles_here] + from_right[0] + from_left[0]
    value_grad = value_acc[tiles_here : 2 * tiles_here] + from_right[1] + from_left[1]
    key_grad, key_gain = norm_back(
        key_hat_grad.reshape(tiles_here, tile_rows, HEADS, HEAD_DIM),
        key_floats,
        key_scale,
        gain_rows[1],
    )
    summed = lax.psum(jnp.stack([query_gain, key_gain]), ("seq", "dp"))
    gain_grads = summed / math.sqrt(
        lax.axis_size("dp") * seq_count * tiles_here * tile_rows * HEADS
    )
    key_low = key_grad.astype(jnp.bfloat16)
    value_low = value_grad.astype(jnp.bfloat16)
    passed = passed_along_2(jnp.stack([query_low, key_low, value_low]), "pipe", -1)
    return (passed[None, :, None], gain_grads[None])


def solution(mesh):
    placed = (
        P("pipe", "dp", "seq", None, None),
        P("pipe", "dp", "seq", None, None),
        P("pipe", "dp", "seq", None, None),
        P("pipe", "dp", "seq", None, None),
        P("pipe", None, None),
        P("pipe", "dp", "seq", None),
    )
    return jax.shard_map(
        local,
        mesh=mesh,
        in_specs=placed,
        out_specs=(P("pipe", None, "dp", "seq", None, None), P("pipe", None, None)),
        check_vma=False,
    )
```

profile of v0, /device:TPU:16, one launch (start us, length us, event | category | flops | bytes accessed | tf_op | source)
XLA Modules:
  0.0 747.3 jit_solution(4585193369530839053)
XLA Ops:
  10.4 5.3 collective-permute-start
  40.4 24.8 %collective-permute-done = bf16[2,1,384,1536]{3,2,1,0:T(8,128)(2,1)} collective-permute-done((bf16[2,1,384,1536]{3,2,1,0:T(8,128)(2,1)}, bf16[2,1,384,1536]{3,2,1,0:T(8,128)(2,1)}, u32[]{:S(2)}, u32[]{:S(2)}) %collective-permute-start) | collective-permute-done | bytes 2359328 | tf_op jit(solution)/shard_map/ppermute | solution.py:19
  65.2 5.5 collective-permute-done.1
  78.4 4.7 gather_fusion.1
  87.6 4.7 gather_fusion
  101.6 5.2 multiply_reduce_fusion.5
  122.2 5.2 multiply_reduce_fusion.4
  143.0 5.2 multiply_reduce_fusion.3
  163.8 5.2 multiply_reduce_fusion.2
  184.6 5.2 multiply_reduce_fusion.1
  202.6 5.0 multiply_reduce_fusion
  297.0 5.0 slice_bitcast_fusion.9
  302.0 4.3 copy.292
  308.3 4.7 copy.289
  322.5 4.3 copy.295
  328.8 4.9 copy.298
  335.7 4.7 copy.301
  342.4 4.7 copy.304
  394.5 6.7 collective-permute-start.3
  420.8 74.6 %collective-permute-done.2 = f32[2,1,384,1536]{3,2,1,0:T(8,128)} collective-permute-done((f32[2,1,384,1536]{3,2,1,0:T(8,128)}, f32[2,1,384,1536]{3,2,1,0:T(8,128)}, u32[]{:S(2)}, u32[]{:S(2)}) %collective-permute-start.2) | collective-permute-done | bytes 4718624 | tf_op jit(solution)/shard_map/ppermute | solution.py:28
  499.0 7.3 fusion.21
  508.3 4.9 multiply_reduce_fusion.8
  522.7 4.5 fusion.65
  552.9 189.6 %psum.7 = f32[2,128]{1,0:T(2,128)S(1)} all-reduce(f32[2,128]{1,0:T(2,128)S(1)} %pad_maximum_fusion.5), channel_id=1, replica_groups=mesh['pipe'=2,'seq'=16,'dp'=4] {'seq','dp'}, use_global_device_ids=true, to_apply=%region_31.32 | all-reduce | flops 256 | bytes 2048 | tf_op jit(solution)/shard_map/psum | solution.py:161
  (313 shorter events, 349.3 us)
Async XLA Ops:
  7.0 15.9 %copy-start.70 = (f32[128]{0:T(128)}, f32[128]{0:T(128)S(1)}, u32[]{:S(2)}) copy-start(f32[128]{0:T(128)S(1)} %get-tuple-element.45) | copy-start | bytes 1540
  8.8 8.3 %copy-start.55 = (bf16[1,1,1,384,1536]{4,3,2,1,0:T(8,128)(2,1)S(1)}, bf16[1,1,1,384,1536]{4,3,2,1,0:T(8,128)(2,1)}, u32[]{:S(2)}) copy-start(bf16[1,1,1,384,1536]{4,3,2,1,0:T(8,128)(2,1)} %param.9) | copy-start | bytes 3538948
  10.4 8.1 %copy-start.7 = (bf16[1,1,1,384,1536]{4,3,2,1,0:T(8,128)(2,1)S(1)}, bf16[1,1,1,384,1536]{4,3,2,1,0:T(8,128)(2,1)}, u32[]{:S(2)}) copy-start(bf16[1,1,1,384,1536]{4,3,2,1,0:T(8,128)(2,1)} %param.6) | copy-start | bytes 3538948
  10.4 54.8 %collective-permute-start = (bf16[2,1,384,1536]{3,2,1,0:T(8,128)(2,1)}, bf16[2,1,384,1536]{3,2,1,0:T(8,128)(2,1)}, u32[]{:S(2)}, u32[]{:S(2)}) collective-permute-start(bf16[2,1,384,1536]{3,2,1,0:T(8,128)(2,1)} %pad_maximum_fusion.4), channel_id=1, source_target_pairs={{0,4},{4,8},{8,12},{12,16},{16,20},{20,24},{24,28},{28,32},{32,36}... | collective-permute-start | bytes 7077896 | tf_op jit(solution)/shard_map/ppermute | solution.py:19
  15.8 54.9 %collective-permute-start.1 = (bf16[2,1,384,1536]{3,2,1,0:T(8,128)(2,1)}, bf16[2,1,384,1536]{3,2,1,0:T(8,128)(2,1)}, u32[]{:S(2)}, u32[]{:S(2)}) collective-permute-start(bf16[2,1,384,1536]{3,2,1,0:T(8,128)(2,1)} %pad_maximum_fusion.4), channel_id=1, source_target_pairs={{4,0},{8,4},{12,8},{16,12},{20,16},{24,20},{28,24},{32,28},{36,32}... | collective-permute-start | bytes 7077896 | tf_op jit(solution)/shard_map/ppermute | solution.py:20
  20.7 380.5 %copy-start = (f32[384,12,128]{0,2,1:T(8,128)}, f32[384,12,128]{0,2,1:T(8,128)S(1)}, u32[]{:S(2)}) copy-start(f32[384,12,128]{0,2,1:T(8,128)S(1)} %mul.607) | copy-start | bytes 7077892
  26.0 44.7 %copy-start.24 = (bf16[1,1,384,1536]{3,2,1,0:T(8,128)(2,1)S(1)}, bf16[1,1,384,1536]{3,2,1,0:T(8,128)(2,1)}, u32[]{:S(2)}) copy-start(bf16[1,1,384,1536]{3,2,1,0:T(8,128)(2,1)} %copy-done.23) | copy-start | bytes 3538948
  36.6 34.1 %copy-start.33 = (bf16[1,1,1,384,1536]{4,3,2,1,0:T(8,128)(2,1)S(1)}, bf16[1,1,1,384,1536]{4,3,2,1,0:T(8,128)(2,1)}, u32[]{:S(2)}) copy-start(bf16[1,1,1,384,1536]{4,3,2,1,0:T(8,128)(2,1)} %param.8) | copy-start | bytes 3538948
  127.5 4.0 copy-start.19
  198.8 8.9 %copy-start.52 = (bf16[1,1152,256]{1,2,0:T(8,128)(2,1)}, bf16[1,1152,256]{1,2,0:T(8,128)(2,1)S(1)}, u32[]{:S(2)}) copy-start(bf16[1,1152,256]{1,2,0:T(8,128)(2,1)S(1)} %copy.364) | copy-start | bytes 1769476
  202.6 5.0 copy-start.54
  207.7 4.0 copy-start.17
  258.2 4.5 copy-start.36
  297.0 5.0 copy-start.34
  390.8 104.6 %collective-permute-start.2 = (f32[2,1,384,1536]{3,2,1,0:T(8,128)}, f32[2,1,384,1536]{3,2,1,0:T(8,128)}, u32[]{:S(2)}, u32[]{:S(2)}) collective-permute-start(f32[2,1,384,1536]{3,2,1,0:T(8,128)} %pad_maximum_fusion.1), channel_id=1, source_target_pairs={{4,0},{8,4},{12,8},{16,12},{20,16},{24,20},{28,24},{32,28},{36,32}... | collective-permute-start | bytes 14155784 | tf_op jit(solution)/shard_map/ppermute | solution.py:28
  394.5 104.5 %collective-permute-start.3 = (f32[2,1,384,1536]{3,2,1,0:T(8,128)}, f32[2,1,384,1536]{3,2,1,0:T(8,128)}, u32[]{:S(2)}, u32[]{:S(2)}) collective-permute-start(f32[2,1,384,1536]{3,2,1,0:T(8,128)} %pad_maximum_fusion.2), channel_id=1, source_target_pairs={{0,4},{4,8},{8,12},{12,16},{16,20},{20,24},{24,28},{28,32},{32,36}... | collective-permute-start | bytes 14155784 | tf_op jit(solution)/shard_map/ppermute | solution.py:28
  410.2 4.3 copy-start.48
  522.6 4.6 copy-start.8
  522.6 4.6 copy-start.25
  522.6 4.8 copy-start.26
  522.6 5.5 copy-start.27
  522.6 6.2 copy-start.28
  522.7 6.2 copy-start.67
  532.1 210.9 %collective-permute-start.4 = (bf16[3,1,384,1536]{3,2,1,0:T(8,128)(2,1)}, bf16[3,1,384,1536]{3,2,1,0:T(8,128)(2,1)}, u32[]{:S(2)}, u32[]{:S(2)}) collective-permute-start(bf16[3,1,384,1536]{3,2,1,0:T(8,128)(2,1)} %pad_maximum_fusion.3), channel_id=1, source_target_pairs={{0,64},{64,0},{1,65},{65,1},{2,66},{66,2},{3,67},{67,3},{4,68},{68... | collective-permute-start | bytes 10616840 | tf_op jit(solution)/shard_map/ppermute | solution.py:34
  (55 other events, 145.2 us)
where the time goes:
time: 754 us; the launch traced here: 747 us
  local copies, waits for them, and re-layouts  235 us (31%)
  blocking collectives  190 us (25%)
  waiting for transfers between devices  109 us (14%)
  other arithmetic  105 us (14%)
  matrix products  91.6 us (12%)
  starting transfers between devices  16.1 us (2%)
    psum x1, blocking collectives, local(): summed = lax.psum(jnp.stack([query_gain, key_gain]), ('seq', 'dp'))  190 us
    ppermute x2, waiting for transfers between devices, passed_along(): lax.ppermute(value, axis, [(source, source + steps) for source in range(i...  78.3 us
    unnamed x172, local copies, waits for them, and re-layouts  58.3 us
    scatter-add x12, other arithmetic, spread(): return totals.at[placed].add(shaped)[:target_span]  39.6 us
    div x6, matrix products, score_block(): attention = exp_scores / totals  31.2 us
    reshape x12, local copies, waits for them, and re-layouts, spread(): slot_grad.reshape(row_count * list_slots, key_rows // list_slots, head_co...  29.8 us
    transpose x6, local copies, waits for them, and re-layouts, tile_pass(): jnp.einsum('nhqk,nqhd->nkhd', attn_low, grad_head, preferred_element_type...  27.7 us
    ppermute x1, waiting for transfers between devices, padded(): before = lax.ppermute(last, axis, up)  24.8 us
  transfers between devices with their start and end apart: 5, of which 4 were waited for; matrix products, arithmetic and copies ran while one was open for 9% of the time, Pallas kernels for 0%

commit v1 on v0

--- a/solution.py
+++ b/solution.py
@@ -158,7 +158,7 @@
         key_scale,
         gain_rows[1],
     )
-    summed = lax.psum(jnp.stack([query_gain, key_gain]), ("seq", "dp"))
+    summed = lax.psum(lax.psum(jnp.stack([query_gain, key_gain]), "dp"), "seq")
     gain_grads = summed / math.sqrt(
         lax.axis_size("dp") * seq_count * tiles_here * tile_rows * HEADS
     )

time: 754 us -> 669 us (0.89)
  blocking collectives: 190 us -> 102 us
    psum x1 -> x2, blocking collectives: 190 us -> 102 us  [local(): summed = lax.psum(lax.psum(jnp.stack([query_gain, key_gain]), 'dp'), 'seq')]
  transfers between devices with their start and end apart: 5 -> 5, of which waited for: 4 -> 4; matrix products, arithmetic and copies ran while one was open for 9% -> 10% of each run, Pallas kernels for 0% -> 0%
where the time goes in v1:
time: 669 us; the launch traced here: 659 us
  local copies, waits for them, and re-layouts  235 us (35%)
  waiting for transfers between devices  108 us (16%)
  other arithmetic  105 us (16%)
  blocking collectives  102 us (15%)
  matrix products  91.6 us (14%)
  starting transfers between devices  16.1 us (2%)
    psum x2, blocking collectives, local(): summed = lax.psum(lax.psum(jnp.stack([query_gain, key_gain]), 'dp'), 'seq')  102 us
    ppermute x2, waiting for transfers between devices, passed_along(): lax.ppermute(value, axis, [(source, source + steps) for source in range(i...  78.1 us
    unnamed x172, local copies, waits for them, and re-layouts  58.2 us
    scatter-add x12, other arithmetic, spread(): return totals.at[placed].add(shaped)[:target_span]  39.6 us
    div x6, matrix products, score_block(): attention = exp_scores / totals  31.3 us
    reshape x12, local copies, waits for them, and re-layouts, spread(): slot_grad.reshape(row_count * list_slots, key_rows // list_slots, head_co...  29.8 us
    transpose x6, local copies, waits for them, and re-layouts, tile_pass(): jnp.einsum('nhqk,nqhd->nkhd', attn_low, grad_head, preferred_element_type...  27.7 us
    ppermute x1, waiting for transfers between devices, padded(): before = lax.ppermute(last, axis, up)  24.8 us
  transfers between devices with their start and end apart: 5, of which 4 were waited for; matrix products, arithmetic and copies ran while one was open for 10% of the time, Pallas kernels for 0%

profile of v1, /device:TPU:16, one launch (start us, length us, event | category | flops | bytes accessed | tf_op | source)
XLA Modules:
  0.0 659.4 jit_solution(4529768686161955279)
XLA Ops:
  10.4 5.3 collective-permute-start
  40.4 24.8 %collective-permute-done = bf16[2,1,384,1536]{3,2,1,0:T(8,128)(2,1)} collective-permute-done((bf16[2,1,384,1536]{3,2,1,0:T(8,128)(2,1)}, bf16[2,1,384,1536]{3,2,1,0:T(8,128)(2,1)}, u32[]{:S(2)}, u32[]{:S(2)}) %collective-permute-start) | collective-permute-done | bytes 2359328 | tf_op jit(solution)/shard_map/ppermute | solution.py:19
  65.2 5.5 collective-permute-done.1
  78.4 4.7 gather_fusion.1
  87.6 4.7 gather_fusion
  101.6 5.2 multiply_reduce_fusion.5
  122.3 5.2 multiply_reduce_fusion.4
  143.0 5.2 multiply_reduce_fusion.3
  163.9 5.2 multiply_reduce_fusion.2
  184.6 5.2 multiply_reduce_fusion.1
  202.7 5.0 multiply_reduce_fusion
  297.1 5.0 slice_bitcast_fusion.9
  302.0 4.3 copy.292
  308.3 4.7 copy.289
  328.9 4.9 copy.298
  335.7 4.7 copy.301
  342.5 4.7 copy.304
  394.6 6.7 %collective-permute-start.3 = (f32[2,1,384,1536]{3,2,1,0:T(8,128)}, f32[2,1,384,1536]{3,2,1,0:T(8,128)}, u32[]{:S(2)}, u32[]{:S(2)}) collective-permute-start(f32[2,1,384,1536]{3,2,1,0:T(8,128)} %pad_maximum_fusion.2), channel_id=1, source_target_pairs={{0,4},{4,8},{8,12},{12,16},{16,20},{20,24},{24,28},{28,32},{32,36}... | collective-permute-start | bytes 14155784 | tf_op jit(solution)/shard_map/ppermute | solution.py:28
  421.1 74.4 %collective-permute-done.2 = f32[2,1,384,1536]{3,2,1,0:T(8,128)} collective-permute-done((f32[2,1,384,1536]{3,2,1,0:T(8,128)}, f32[2,1,384,1536]{3,2,1,0:T(8,128)}, u32[]{:S(2)}, u32[]{:S(2)}) %collective-permute-start.2) | collective-permute-done | bytes 4718624 | tf_op jit(solution)/shard_map/ppermute | solution.py:28
  499.1 7.3 %fusion.21 = (f32[1,384,1536]{2,1,0:T(8,128)S(1)}, bf16[1,1,384,1536]{3,2,1,0:T(8,128)(2,1)}) fusion(f32[2,1,384,1536]{3,2,1,0:T(8,128)} %collective-permute-done.3, f32[2,1,384,1536]{3,2,1,0:T(8,128)} %collective-permute-done.2, f32[3,384,1536]{2,1,0:T(8,128)} %slice_dynamic-update-slice_fusion.6, f32[3,384,1536]{2,1,0:T(8,128)} %slice_dynamic-update-slice_fusion), kind=kLoop, calls=%fused_computation.80 | loop fusion | flops 2949120 | bytes 17694720 | tf_op jit(solution)/shard_map/add | solution.py:153
  508.4 4.9 multiply_reduce_fusion.8
  522.7 4.5 fusion.65
  552.9 59.3 %psum.14 = f32[2,128]{1,0:T(2,128)S(1)} all-reduce(f32[2,128]{1,0:T(2,128)S(1)} %pad_maximum_fusion.5), channel_id=1, replica_groups=mesh['pipe'=2,'seq'=16,'dp'=4] {'dp'}, use_global_device_ids=true, to_apply=%region_31.32 | all-reduce | flops 256 | bytes 2048 | tf_op jit(solution)/shard_map/psum | solution.py:161
  612.2 42.3 %psum.15 = f32[2,128]{1,0:T(2,128)S(1)} all-reduce(f32[2,128]{1,0:T(2,128)S(1)} %psum.14), channel_id=1, replica_groups=mesh['pipe'=2,'seq'=16,'dp'=4] {'seq'}, use_global_device_ids=true, to_apply=%region_32.33 | all-reduce | flops 256 | bytes 2048 | tf_op jit(solution)/shard_map/psum | solution.py:161
  (314 shorter events, 353.9 us)
Async XLA Ops:
  7.0 15.9 %copy-start.70 = (f32[128]{0:T(128)}, f32[128]{0:T(128)S(1)}, u32[]{:S(2)}) copy-start(f32[128]{0:T(128)S(1)} %get-tuple-element.45) | copy-start | bytes 1540
  8.8 8.3 %copy-start.55 = (bf16[1,1,1,384,1536]{4,3,2,1,0:T(8,128)(2,1)S(1)}, bf16[1,1,1,384,1536]{4,3,2,1,0:T(8,128)(2,1)}, u32[]{:S(2)}) copy-start(bf16[1,1,1,384,1536]{4,3,2,1,0:T(8,128)(2,1)} %param.9) | copy-start | bytes 3538948
  10.4 8.1 %copy-start.7 = (bf16[1,1,1,384,1536]{4,3,2,1,0:T(8,128)(2,1)S(1)}, bf16[1,1,1,384,1536]{4,3,2,1,0:T(8,128)(2,1)}, u32[]{:S(2)}) copy-start(bf16[1,1,1,384,1536]{4,3,2,1,0:T(8,128)(2,1)} %param.6) | copy-start | bytes 3538948
  10.4 54.8 %collective-permute-start = (bf16[2,1,384,1536]{3,2,1,0:T(8,128)(2,1)}, bf16[2,1,384,1536]{3,2,1,0:T(8,128)(2,1)}, u32[]{:S(2)}, u32[]{:S(2)}) collective-permute-start(bf16[2,1,384,1536]{3,2,1,0:T(8,128)(2,1)} %pad_maximum_fusion.4), channel_id=1, source_target_pairs={{0,4},{4,8},{8,12},{12,16},{16,20},{20,24},{24,28},{28,32},{32,36}... | collective-permute-start | bytes 7077896 | tf_op jit(solution)/shard_map/ppermute | solution.py:19
  15.8 54.9 %collective-permute-start.1 = (bf16[2,1,384,1536]{3,2,1,0:T(8,128)(2,1)}, bf16[2,1,384,1536]{3,2,1,0:T(8,128)(2,1)}, u32[]{:S(2)}, u32[]{:S(2)}) collective-permute-start(bf16[2,1,384,1536]{3,2,1,0:T(8,128)(2,1)} %pad_maximum_fusion.4), channel_id=1, source_target_pairs={{4,0},{8,4},{12,8},{16,12},{20,16},{24,20},{28,24},{32,28},{36,32}... | collective-permute-start | bytes 7077896 | tf_op jit(solution)/shard_map/ppermute | solution.py:20
  20.7 380.6 %copy-start = (f32[384,12,128]{0,2,1:T(8,128)}, f32[384,12,128]{0,2,1:T(8,128)S(1)}, u32[]{:S(2)}) copy-start(f32[384,12,128]{0,2,1:T(8,128)S(1)} %mul.607) | copy-start | bytes 7077892
  26.0 44.7 %copy-start.24 = (bf16[1,1,384,1536]{3,2,1,0:T(8,128)(2,1)S(1)}, bf16[1,1,384,1536]{3,2,1,0:T(8,128)(2,1)}, u32[]{:S(2)}) copy-start(bf16[1,1,384,1536]{3,2,1,0:T(8,128)(2,1)} %copy-done.23) | copy-start | bytes 3538948
  36.6 34.1 %copy-start.33 = (bf16[1,1,1,384,1536]{4,3,2,1,0:T(8,128)(2,1)S(1)}, bf16[1,1,1,384,1536]{4,3,2,1,0:T(8,128)(2,1)}, u32[]{:S(2)}) copy-start(bf16[1,1,1,384,1536]{4,3,2,1,0:T(8,128)(2,1)} %param.8) | copy-start | bytes 3538948
  127.5 4.0 copy-start.19
  189.9 4.0 copy-start.22
  198.9 8.9 %copy-start.52 = (bf16[1,1152,256]{1,2,0:T(8,128)(2,1)}, bf16[1,1152,256]{1,2,0:T(8,128)(2,1)S(1)}, u32[]{:S(2)}) copy-start(bf16[1,1152,256]{1,2,0:T(8,128)(2,1)S(1)} %copy.364) | copy-start | bytes 1769476
  202.7 5.0 copy-start.54
  258.3 4.5 copy-start.36
  297.1 5.0 copy-start.34
  390.8 104.6 %collective-permute-start.2 = (f32[2,1,384,1536]{3,2,1,0:T(8,128)}, f32[2,1,384,1536]{3,2,1,0:T(8,128)}, u32[]{:S(2)}, u32[]{:S(2)}) collective-permute-start(f32[2,1,384,1536]{3,2,1,0:T(8,128)} %pad_maximum_fusion.1), channel_id=1, source_target_pairs={{4,0},{8,4},{12,8},{16,12},{20,16},{24,20},{28,24},{32,28},{36,32}... | collective-permute-start | bytes 14155784 | tf_op jit(solution)/shard_map/ppermute | solution.py:28
  394.6 104.5 %collective-permute-start.3 = (f32[2,1,384,1536]{3,2,1,0:T(8,128)}, f32[2,1,384,1536]{3,2,1,0:T(8,128)}, u32[]{:S(2)}, u32[]{:S(2)}) collective-permute-start(f32[2,1,384,1536]{3,2,1,0:T(8,128)} %pad_maximum_fusion.2), channel_id=1, source_target_pairs={{0,4},{4,8},{8,12},{12,16},{16,20},{20,24},{24,28},{28,32},{32,36}... | collective-permute-start | bytes 14155784 | tf_op jit(solution)/shard_map/ppermute | solution.py:28
  410.4 4.3 copy-start.48
  522.7 4.6 copy-start.8
  522.7 4.6 copy-start.25
  522.7 4.8 copy-start.26
  522.7 5.5 copy-start.27
  522.7 6.2 copy-start.28
  522.7 6.2 copy-start.67
  532.1 123.0 %collective-permute-start.4 = (bf16[3,1,384,1536]{3,2,1,0:T(8,128)(2,1)}, bf16[3,1,384,1536]{3,2,1,0:T(8,128)(2,1)}, u32[]{:S(2)}, u32[]{:S(2)}) collective-permute-start(bf16[3,1,384,1536]{3,2,1,0:T(8,128)(2,1)} %pad_maximum_fusion.3), channel_id=1, source_target_pairs={{0,64},{64,0},{1,65},{65,1},{2,66},{66,2},{3,67},{67,3},{4,68},{68... | collective-permute-start | bytes 10616840 | tf_op jit(solution)/shard_map/ppermute | solution.py:34
  (55 other events, 145.4 us)
